TPU v7x, 32 devices: a whole 2x2x4 slice. The times are simulated.
32 devices in a mesh: obj: 8 (over z, y), blk: 4 (over x, core).
Axes of the slice: x: 2, y: 2, z: 4, core: 2. Of those that a mesh axis runs over, the one named last changes fastest.
Arguments:
- tokens: bfloat16 [8, 3072, 512], P('obj', 'blk'), may hold values from -6 to 6
- context: bfloat16 [8, 581, 384], P('obj'), may hold values from -6 to 6
- camera_groups: int32 [8], P('obj'), may hold values from 0 to 7
- camera_table: bfloat16 [8, 1024], replicated, may hold values from -6 to 6
- cross_query: bfloat16 [512, 512], replicated, may hold values from -0.25 to 0.25
- cross_kv: bfloat16 [384, 1024], replicated, may hold values from -0.3125 to 0.3125
- cross_out: bfloat16 [512, 512], replicated, may hold values from -4 to 4
- self_qkv: bfloat16 [512, 1536], replicated, may hold values from -0.25 to 0.25
- self_out: bfloat16 [512, 512], replicated, may hold values from -6 to 6
- mlp_up: bfloat16 [512, 2048], replicated, may hold values from -0.25 to 0.25
- mlp_down: bfloat16 [2048, 512], replicated, may hold values from -0.125 to 0.125
- norm_gain: bfloat16 [3, 512], replicated, may hold values from 0.25 to 1.75
- norm_bias: bfloat16 [3, 512], replicated, may hold values from -4 to 4
- mod_weight: bfloat16 [3, 1024, 1024], replicated, may hold values from -0.09375 to 0.09375
- mod_bias: bfloat16 [3, 1024], replicated, may hold values from -4 to 4
- cotangent: bfloat16 [8, 3072, 512], P('obj', 'blk'), may hold values from -6 to 6
Outputs:
- mixed: bfloat16 [8, 3072, 512], P('obj', 'blk')
- tokens_grad: float32 [8, 3072, 512], P('obj', 'blk')
- context_grad: float32 [8, 581, 384], P('obj')
- cross_query_grad: float32 [512, 512], P(None, 'blk')
- cross_kv_grad: float32 [384, 1024], P(None, 'blk')
- cross_out_grad: float32 [512, 512], P(None, 'blk')
- self_qkv_grad: float32 [512, 1536], P(None, 'blk')
- self_out_grad: float32 [512, 512], P(None, 'blk')
- mlp_up_grad: float32 [512, 2048], P(None, 'blk')
- mlp_down_grad: float32 [2048, 512], P(None, 'blk')
- norm_gain_grad: float32 [3, 512], P(None, 'blk')
- norm_bias_grad: float32 [3, 512], P(None, 'blk')
- mod_weight_grad: float32 [3, 1024, 1024], P(None, None, 'blk')
- mod_bias_grad: float32 [3, 1024], P(None, 'blk')
All inputs are finite; a program needn't handle non-finite values.
Results may differ from a plain program's by a relative error of at most 0.02.
Values may be sent and summed in bfloat16 or wider, within the bound.
A program may use at most 320 MiB of HBM per device.

v0:
```python
import jax
import jax.numpy as jnp
from jax import lax
from jax.sharding import PartitionSpec as P

D = 512
HEADS = 8
HEAD_DIM = 64


epsilon = 1e-06
highest = lax.Precision.HIGHEST


def from_behind(block, axis, distance):
    devices = range(lax.axis_size(axis))
    route = [((i - distance) % len(devices), i) for i in devices]
    return lax.ppermute(block, axis, route)


def head_split(array):
    return array.reshape(array.shape[0], array.shape[1], HEADS, HEAD_DIM)


def flatten_heads(array):
    return array.reshape(array.shape[0], array.shape[1], D)


def score_rows(queries, key_rows):
    product = jnp.einsum(
        "oshd,okhd->ohsk",
        head_split(queries),
        head_split(key_rows),
        preferred_element_type=jnp.float32,
    )
    return product * HEAD_DIM ** (-0.5)


def modulate(inputs, gain_row, offset, shift_row, scale_row):
    center = inputs - jnp.mean(inputs, -1, keepdims=True)
    inverse = lax.rsqrt(jnp.mean(center * center, -1, keepdims=True) + epsilon)
    normed = center * inverse
    affine = normed * gain_row + offset
    result = affine * (1.0 + scale_row[:, None, :]) + shift_row[:, None, :]
    return (result, (normed, inverse, affine))


def modulate_back(incoming, saved, gain_row, scale_row):
    normed, inverse, affine = saved
    shift_grad = jnp.sum(incoming, 1)
    scale_grad = jnp.sum(incoming * affine, 1)
    affine_grad = incoming * (1.0 + scale_row[:, None, :])
    gain_grad = jnp.sum(affine_grad * normed, (0, 1))
    offset_grad = jnp.sum(affine_grad, (0, 1))
    normed_grad = affine_grad * gain_row
    input_grad = inverse * (
        normed_grad
        - jnp.mean(normed_grad, -1, keepdims=True)
        - normed * jnp.mean(normed_grad * normed, -1, keepdims=True)
    )
    return (input_grad, jnp.concatenate([shift_grad, scale_grad], -1), gain_grad, offset_grad)


def absorb(state, queries, key_pair):
    run_max, run_sum, run_out = state
    scores = score_rows(queries, key_pair[..., :D])
    new_max = jnp.maximum(run_max, jnp.max(scores, -1))
    weights = jnp.exp(scores - new_max[..., None])
    run_sum = jnp.sum(weights, -1)
    merged = jnp.einsum(
        "ohsk,okhd->oshd",
        weights.astype(jnp.bfloat16),
        head_split(key_pair[..., D:]),
        preferred_element_type=jnp.float32,
    )
    run_out = merged
    return (new_max, run_sum, run_out)


def finish(state):
    run_max, run_sum, run_out = state
    output = run_out / jnp.transpose(run_sum, (0, 2, 1))[..., None]
    return (flatten_heads(output), run_max + jnp.log(run_sum))


def row_delta(grad_low, output):
    product = head_split(grad_low.astype(jnp.float32)) * head_split(output)
    return jnp.transpose(jnp.sum(product, -1), (0, 2, 1))


def attention_back(queries, key_pair, grad_out, logsum, delta):
    key_rows = key_pair[..., :D]
    value_rows = key_pair[..., D:]
    probs = jnp.exp(score_rows(queries, key_rows) - logsum[..., None])
    probs_grad = jnp.einsum(
        "oshd,okhd->ohsk",
        head_split(grad_out),
        head_split(value_rows),
        preferred_element_type=jnp.float32,
    )
    scores_grad = (probs * (probs_grad - delta[..., None])).astype(jnp.bfloat16)
    factor = HEAD_DIM ** (-0.5)
    query_grad = (
        jnp.einsum(
            "ohsk,okhd->oshd", scores_grad, head_split(key_rows), preferred_element_type=jnp.float32
        )
        * factor
    )
    key_grad = (
        jnp.einsum(
            "ohsk,oshd->okhd", scores_grad, head_split(queries), preferred_element_type=jnp.float32
        )
        * factor
    )
    value_grad = jnp.einsum(
        "ohsk,oshd->okhd",
        probs.astype(jnp.bfloat16),
        head_split(grad_out),
        preferred_element_type=jnp.float32,
    )
    return (
        flatten_heads(query_grad),
        jnp.concatenate([flatten_heads(key_grad), flatten_heads(value_grad)], -1),
    )


def pass_pair(key_pair):
    return from_behind(key_pair, "blk", 1)


def pass_owed(owed_grad):
    return from_behind(owed_grad.astype(jnp.bfloat16), "blk", 1).astype(owed_grad.dtype)


def body(
    tokens,
    context,
    camera_groups,
    camera_table,
    cross_query,
    cross_kv,
    cross_out,
    self_qkv,
    self_out,
    mlp_up,
    mlp_down,
    norm_gain,
    norm_bias,
    mod_weight,
    mod_bias,
    cotangent,
):
    object_count = tokens.shape[0]
    length = tokens.shape[1]
    cycle_size = lax.axis_size("blk")
    picked = (
        camera_groups[:, None] == jnp.arange(camera_table.shape[0], dtype=jnp.int32)[None, :]
    ).astype(jnp.bfloat16)
    camera = jnp.dot(picked, camera_table, preferred_element_type=jnp.float32)
    lifted = jax.nn.silu(camera).astype(jnp.bfloat16)
    modulation = jnp.einsum(
        "oc,jcm->ojm", lifted, mod_weight, preferred_element_type=jnp.float32
    ) + mod_bias.astype(jnp.float32)
    gains = norm_gain.astype(jnp.float32)
    offsets = norm_bias.astype(jnp.float32)

    def norm_at(inputs, position):
        return modulate(
            inputs,
            gains[position],
            offsets[position],
            modulation[:, position, :D],
            modulation[:, position, D:],
        )

    initial = (
        jnp.full((object_count, HEADS, length), -1e30, jnp.float32),
        jnp.zeros((object_count, HEADS, length), jnp.float32),
        jnp.zeros((object_count, length, HEADS, HEAD_DIM), jnp.float32),
    )
    start_rows = tokens.astype(jnp.float32)
    normed_one, saved_one = norm_at(start_rows, 0)
    first_in = normed_one.astype(jnp.bfloat16)
    cross_q = jnp.einsum(
        "osd,de->ose", first_in, cross_query, preferred_element_type=jnp.float32
    ).astype(jnp.bfloat16)
    cross_pair = jnp.einsum(
        "ocw,we->oce", context, cross_kv, preferred_element_type=jnp.float32
    ).astype(jnp.bfloat16)
    cross_att, cross_log = finish(absorb(initial, cross_q, cross_pair))
    cross_low = cross_att.astype(jnp.bfloat16)
    after_one = start_rows + jnp.einsum(
        "osd,de->ose", cross_low, cross_out, preferred_element_type=jnp.float32
    )
    normed_two, saved_two = norm_at(after_one, 1)
    second_in = normed_two.astype(jnp.bfloat16)
    joint_rows = jnp.einsum(
        "osd,de->ose", second_in, self_qkv, preferred_element_type=jnp.float32
    ).astype(jnp.bfloat16)
    self_q = joint_rows[..., :D]
    own_pair = joint_rows[..., D:]
    begin = (initial,)
    self_att, self_log = finish(
        absorb(begin[0], self_q, lax.all_gather(own_pair, "blk", axis=1, tiled=True))
    )
    self_low = self_att.astype(jnp.bfloat16)
    after_two = after_one + jnp.einsum(
        "osd,de->ose", self_low, self_out, preferred_element_type=jnp.float32
    )
    normed_three, saved_three = norm_at(after_two, 2)
    third_in = normed_three.astype(jnp.bfloat16)
    hidden = jnp.einsum("osd,df->osf", third_in, mlp_up, preferred_element_type=jnp.float32)
    active, gelu_pull = jax.vjp(jax.nn.gelu, hidden)
    active_low = active.astype(jnp.bfloat16)
    final_rows = after_two + jnp.einsum(
        "osf,fd->osd", active_low, mlp_down, preferred_element_type=jnp.float32
    )
    mixed = final_rows.astype(jnp.bfloat16)
    grad_three = cotangent.astype(jnp.float32)
    down_grad = jnp.einsum("osf,osd->fd", active_low, cotangent, preferred_element_type=jnp.float32)
    active_grad = jnp.einsum("osd,fd->osf", cotangent, mlp_down, preferred_element_type=jnp.float32)
    hidden_grad = gelu_pull(active_grad)[0].astype(jnp.bfloat16)
    up_grad = jnp.einsum("osd,osf->df", third_in, hidden_grad, preferred_element_type=jnp.float32)
    norm_three_grad = jnp.einsum(
        "osf,df->osd", hidden_grad, mlp_up, preferred_element_type=jnp.float32
    )
    back_three, mode_three, gain_three, offset_three = modulate_back(
        norm_three_grad, saved_three, gains[2], modulation[:, 2, D:]
    )
    grad_two = grad_three + back_three
    self_grad = grad_two.astype(jnp.bfloat16)
    sout_grad = jnp.einsum("osd,ose->de", self_low, self_grad, preferred_element_type=jnp.float32)
    att_grad = jnp.einsum(
        "ose,de->osd", self_grad, self_out, preferred_element_type=jnp.float32
    ).astype(jnp.bfloat16)
    self_delta = row_delta(att_grad, self_att)
    zero_pair = jnp.zeros((object_count, length, 2 * D), jnp.float32)
    zero_query = jnp.zeros((object_count, length, D), jnp.float32)

    def key_turn(turn_index, carried):
        key_pair, owed_grad, query_grad = carried
        part_query, part_pair = attention_back(self_q, key_pair, att_grad, self_log, self_delta)
        return (pass_pair(key_pair), pass_owed(owed_grad + part_pair), query_grad + part_query)

    key_pair, owed_grad, query_grad = lax.fori_loop(
        0, cycle_size - 1, key_turn, (own_pair, zero_pair, zero_query)
    )
    part_query, part_pair = attention_back(self_q, key_pair, att_grad, self_log, self_delta)
    joint_grad = jnp.concatenate([query_grad + part_query, pass_owed(owed_grad + part_pair)], -1)
    joint_low = joint_grad.astype(jnp.bfloat16)
    qkv_grad = jnp.einsum("osd,ose->de", second_in, joint_low, preferred_element_type=jnp.float32)
    norm_two_grad = jnp.einsum(
        "ose,de->osd", joint_low, self_qkv, preferred_element_type=jnp.float32
    )
    back_two, mode_two, gain_two, offset_two = modulate_back(
        norm_two_grad, saved_two, gains[1], modulation[:, 1, D:]
    )
    grad_one = grad_two + back_two
    cross_grad = grad_one.astype(jnp.bfloat16)
    cout_grad = jnp.einsum("osd,ose->de", cross_low, cross_grad, preferred_element_type=jnp.float32)
    catt_grad = jnp.einsum(
        "ose,de->osd", cross_grad, cross_out, preferred_element_type=jnp.float32
    ).astype(jnp.bfloat16)
    cross_delta = row_delta(catt_grad, cross_att)
    cross_qgrad, cross_pgrad = attention_back(
        cross_q, cross_pair, catt_grad, cross_log, cross_delta
    )
    cross_qlow = cross_qgrad.astype(jnp.bfloat16)
    cq_grad = jnp.einsum("osd,ose->de", first_in, cross_qlow, preferred_element_type=jnp.float32)
    norm_one_grad = jnp.einsum(
        "ose,de->osd", cross_qlow, cross_query, preferred_element_type=jnp.float32
    )
    back_one, mode_one, gain_one, offset_one = modulate_back(
        norm_one_grad, saved_one, gains[0], modulation[:, 0, D:]
    )
    tokens_grad = grad_one + back_one
    pair_low = lax.psum(cross_pgrad.astype(jnp.bfloat16), "blk")
    context_grad = jnp.einsum("oce,we->ocw", pair_low, cross_kv, preferred_element_type=jnp.float32)
    column_width = 2 * D // cycle_size
    column_rows = lax.dynamic_slice_in_dim(
        pair_low, lax.axis_index("blk") * column_width, column_width, 2
    )
    ckv_grad = jnp.einsum("ocw,oce->we", context, column_rows, preferred_element_type=jnp.float32)
    mode_grads = jnp.stack([mode_one, mode_two, mode_three], 1)
    gain_grads = jnp.stack([gain_one, gain_two, gain_three], 0)
    offset_grads = jnp.stack([offset_one, offset_two, offset_three], 0)
    modb_grad = jnp.sum(mode_grads, 0)
    lifted_wide = lifted.astype(jnp.float32)
    cam_width = mod_weight.shape[1]
    modw_grad = jnp.einsum("oc,ojm->jcm", lifted_wide, mode_grads, precision=highest)
    shares = (
        lax.psum_scatter(
            cq_grad.astype(jnp.bfloat16), "blk", scatter_dimension=1, tiled=True
        ).astype(jnp.float32),
        lax.psum_scatter(
            cout_grad.astype(jnp.bfloat16), "blk", scatter_dimension=1, tiled=True
        ).astype(jnp.float32),
        lax.psum_scatter(
            qkv_grad.astype(jnp.bfloat16), "blk", scatter_dimension=1, tiled=True
        ).astype(jnp.float32),
        lax.psum_scatter(
            sout_grad.astype(jnp.bfloat16), "blk", scatter_dimension=1, tiled=True
        ).astype(jnp.float32),
        lax.psum_scatter(
            up_grad.astype(jnp.bfloat16), "blk", scatter_dimension=1, tiled=True
        ).astype(jnp.float32),
        lax.psum_scatter(
            down_grad.astype(jnp.bfloat16), "blk", scatter_dimension=1, tiled=True
        ).astype(jnp.float32),
        lax.psum_scatter(
            gain_grads.astype(jnp.bfloat16), "blk", scatter_dimension=1, tiled=True
        ).astype(jnp.float32),
        lax.psum_scatter(
            offset_grads.astype(jnp.bfloat16), "blk", scatter_dimension=1, tiled=True
        ).astype(jnp.float32),
        lax.psum_scatter(
            modw_grad.reshape(3 * cam_width, 2 * D).astype(jnp.bfloat16),
            "blk",
            scatter_dimension=1,
            tiled=True,
        ).astype(jnp.float32),
        lax.psum_scatter(
            modb_grad.astype(jnp.bfloat16), "blk", scatter_dimension=1, tiled=True
        ).astype(jnp.float32),
    )
    totals = (
        lax.psum(shares[0].astype(jnp.bfloat16), "obj").astype(jnp.float32),
        lax.psum(shares[1].astype(jnp.bfloat16), "obj").astype(jnp.float32),
        lax.psum(shares[2].astype(jnp.bfloat16), "obj").astype(jnp.float32),
        lax.psum(shares[3].astype(jnp.bfloat16), "obj").astype(jnp.float32),
        lax.psum(shares[4].astype(jnp.bfloat16), "obj").astype(jnp.float32),
        lax.psum(shares[5].astype(jnp.bfloat16), "obj").astype(jnp.float32),
        lax.psum(shares[6].astype(jnp.bfloat16), "obj").astype(jnp.float32),
        lax.psum(shares[7].astype(jnp.bfloat16), "obj").astype(jnp.float32),
        lax.psum(shares[8].astype(jnp.bfloat16), "obj").astype(jnp.float32),
        lax.psum(shares[9].astype(jnp.bfloat16), "obj").astype(jnp.float32),
        lax.psum(ckv_grad.astype(jnp.bfloat16), "obj").astype(jnp.float32),
    )
    mod_weight_grad = totals[8].reshape(3, cam_width, column_width)
    mod_bias_grad = totals[9]
    cross_kv_grad = totals[10]
    return (
        mixed,
        tokens_grad,
        context_grad,
        totals[0],
        cross_kv_grad,
        totals[1],
        totals[2],
        totals[3],
        totals[4],
        totals[5],
        totals[6],
        totals[7],
        mod_weight_grad,
        mod_bias_grad,
    )


def solution(mesh):
    placed = (
        P("obj", "blk", None),
        P("obj", None, None),
        P("obj"),
        P(),
        P(),
        P(),
        P(),
        P(),
        P(),
        P(),
        P(),
        P(),
        P(),
        P(),
        P(),
        P("obj", "blk", None),
    )
    return jax.shard_map(
        body,
        mesh=mesh,
        in_specs=placed,
        out_specs=(
            P("obj", "blk", None),
            P("obj", "blk", None),
            P("obj", None, None),
            P(None, "blk"),
            P(None, "blk"),
            P(None, "blk"),
            P(None, "blk"),
            P(None, "blk"),
            P(None, "blk"),
            P(None, "blk"),
            P(None, "blk"),
            P(None, "blk"),
            P(None, None, "blk"),
            P(None, "blk"),
        ),
        check_vma=False,
    )
```

profile of v0, /device:TPU:0, one launch (start us, length us, event | category | flops | bytes accessed | tf_op | source)
XLA Modules:
  0.0 1010.0 jit_solution(14607053492542865059)
XLA Ops:
  21.8 7.2 multiply_reduce_fusion.1
  31.0 7.7 fusion.10
  38.7 9.0 fusion.121
  64.0 40.8 %all-gather.2.cloned.1.call-done = bf16[1,3072,1024]{2,1,0:T(8,128)(2,1)} async-done(((bf16[1,768,1024]{2,1,0:T(8,128)(2,1)}), bf16[1,3072,1024]{2,1,0:T(8,128)(2,1)}) %all-gather.2.cloned.1.call-update) | async-done | bytes 6291472 | tf_op jit(solution)/shard_map/all_gather | solution.py:204
  104.8 6.0 fusion.116
  110.8 4.7 copy.79
  115.4 28.9 %multiply_reduce_fusion = (f32[8,768]{1,0:T(8,128)S(1)}, f32[8,768,3072]{2,1,0:T(8,128)}) fusion(bf16[768,8,64]{0,2,1:T(8,128)(2,1)S(1)} %bitcast.364, bf16[3072,8,64]{0,2,1:T(8,128)(2,1)} %bitcast.385), kind=kOutput, calls=%fused_computation.11 | convolution fusion | flops 2453661696 | bytes 79454208 | tf_op jit(solution)/shard_map/oshd,okhd->ohsk/dot_general | solution.py:30
  144.3 4.6 copy.77
  149.0 23.8 %fusion.5 = f32[8,768]{1,0:T(8,128)S(1)} fusion(f32[8,768,3072]{2,1,0:T(8,128)} %get-tuple-element.225, f32[8,768]{1,0:T(8,128)S(1)} %broadcast_maximum_fusion), kind=kLoop, calls=%fused_computation.12 | loop fusion | flops 56616960 | bytes 75546624 | tf_op jit(solution)/shard_map/reduce_sum | solution.py:69
  172.8 28.8 %fusion.123 = (bf16[1,768,8,64]{1,3,2,0:T(8,128)(2,1)}, f32[1,768,8,64]{1,3,2,0:T(8,128)}) fusion(f32[768,8]{0,1:T(8,128)S(1)} %bitcast.406, bf16[3072,8,64]{0,2,1:T(8,128)(2,1)} %bitcast.384, f32[8,768,3072]{2,1,0:T(8,128)} %get-tuple-element.225, f32[8,768]{1,0:T(8,128)S(1)} %broadcast_maximum_fusion), kind=kOutput, calls=%fused_computation.205 | convolution fusion | flops 2473328640 | bytes 81051648 | tf_op jit(solution)/shard_map/ohsk,okhd->oshd/dot_general | solution.py:70
  207.3 5.3 fusion.29
  226.8 216.1 %while.15 = (s32[]{:T(128)}, bf16[1,768,1024]{1,2,0:T(8,128)(2,1)}, f32[1,768,1024]{1,2,0:T(8,128)}, f32[1,768,512]{1,2,0:T(8,128)}, bf16[1,768,512]{1,2,0:T(8,1...) while((s32[]{:T(128)}, bf16[1,768,1024]{1,2,0:T(8,128)(2,1)}, ...), condition=%wide.region_14.15_spmd.clone, body=%wide.region_13.14_spmd.clone.sunk | while | flops 3063152640 | bytes 257237312 | solution.py:245
  234.8 6.3 fusion.213
  241.8 9.5 multiply_convert_fusion.11
  261.8 6.7 convolution_multiply_fusion.8
  268.9 12.6 %collective-permute-done.1 = bf16[1,768,1024]{1,2,0:T(8,128)(2,1)} collective-permute-done((bf16[1,768,1024]{1,2,0:T(8,128)(2,1)}, bf16[1,768,1024]{1,2,0:T(8,128)(2,1)}, u32[]{:S(2)}, u32[]{:S(2)}) %collective-permute-start.1) | collective-permute-done | bytes 1572896 | tf_op jit(solution)/shard_map/while/body/eval_jaxpr/ppermute | solution.py:18
  284.8 13.5 %collective-permute-done = bf16[1,768,1024]{1,2,0:T(8,128)(2,1)} collective-permute-done((bf16[1,768,1024]{1,2,0:T(8,128)(2,1)}, bf16[1,768,1024]{1,2,0:T(8,128)(2,1)}, u32[]{:S(2)}, u32[]{:S(2)}) %collective-permute-start) | collective-permute-done | bytes 1572896 | tf_op jit(solution)/shard_map/while/body/eval_jaxpr/ppermute | solution.py:18
  306.1 6.3 fusion.213
  313.1 9.5 multiply_convert_fusion.11
  334.1 6.7 convolution_multiply_fusion.8
  341.2 12.6 %collective-permute-done.1 = bf16[1,768,1024]{1,2,0:T(8,128)(2,1)} collective-permute-done((bf16[1,768,1024]{1,2,0:T(8,128)(2,1)}, bf16[1,768,1024]{1,2,0:T(8,128)(2,1)}, u32[]{:S(2)}, u32[]{:S(2)}) %collective-permute-start.1) | collective-permute-done | bytes 1572896 | tf_op jit(solution)/shard_map/while/body/eval_jaxpr/ppermute | solution.py:18
  357.1 13.5 %collective-permute-done = bf16[1,768,1024]{1,2,0:T(8,128)(2,1)} collective-permute-done((bf16[1,768,1024]{1,2,0:T(8,128)(2,1)}, bf16[1,768,1024]{1,2,0:T(8,128)(2,1)}, u32[]{:S(2)}, u32[]{:S(2)}) %collective-permute-start) | collective-permute-done | bytes 1572896 | tf_op jit(solution)/shard_map/while/body/eval_jaxpr/ppermute | solution.py:18
  378.4 6.3 fusion.213
  385.4 9.5 multiply_convert_fusion.11
  406.3 6.7 convolution_multiply_fusion.8
  413.5 12.6 %collective-permute-done.1 = bf16[1,768,1024]{1,2,0:T(8,128)(2,1)} collective-permute-done((bf16[1,768,1024]{1,2,0:T(8,128)(2,1)}, bf16[1,768,1024]{1,2,0:T(8,128)(2,1)}, u32[]{:S(2)}, u32[]{:S(2)}) %collective-permute-start.1) | collective-permute-done | bytes 1572896 | tf_op jit(solution)/shard_map/while/body/eval_jaxpr/ppermute | solution.py:18
  429.4 13.5 %collective-permute-done = bf16[1,768,1024]{1,2,0:T(8,128)(2,1)} collective-permute-done((bf16[1,768,1024]{1,2,0:T(8,128)(2,1)}, bf16[1,768,1024]{1,2,0:T(8,128)(2,1)}, u32[]{:S(2)}, u32[]{:S(2)}) %collective-permute-start) | collective-permute-done | bytes 1572896 | tf_op jit(solution)/shard_map/while/body/eval_jaxpr/ppermute | solution.py:18
  447.9 6.4 fusion.13
  454.9 9.3 multiply_convert_fusion.1
  474.0 6.7 convolution_multiply_fusion.3
  480.9 10.8 %collective-permute-done.2 = bf16[1,768,1024]{1,2,0:T(8,128)(2,1)} collective-permute-done((bf16[1,768,1024]{1,2,0:T(8,128)(2,1)}, bf16[1,768,1024]{1,2,0:T(8,128)(2,1)}, u32[]{:S(2)}, u32[]{:S(2)}) %collective-permute-start.2) | collective-permute-done | bytes 1572896 | tf_op jit(solution)/shard_map/ppermute | solution.py:18
  491.7 4.7 fusion.126
  507.4 9.3 multiply_convert_fusion.2
  516.7 5.7 fusion.70
  537.1 7.1 convolution_convert_fusion.1
  557.3 5.2 convolution_convert_fusion.2
  572.0 5.0 multiply_convert_fusion.3
  591.9 23.0 %reduce-scatter.33.cloned.1.call-done = bf16[128,512]{1,0:T(8,128)(2,1)} async-done(((bf16[512,512]{1,0:T(8,128)(2,1)}), bf16[128,512]{1,0:T(8,128)(2,1)}) %reduce-scatter.33.cloned.1.call-update) | async-done | bytes 131088
  616.5 32.3 %reduce-scatter.39.cloned.1.call-done = bf16[128,2048]{1,0:T(8,128)(2,1)} async-done(((bf16[512,2048]{1,0:T(8,128)(2,1)}), bf16[128,2048]{1,0:T(8,128)(2,1)}) %reduce-scatter.39.cloned.1.call-update) | async-done | bytes 524304
  650.9 28.7 %reduce-scatter.35.cloned.1.call-done = bf16[384,512]{1,0:T(8,128)(2,1)} async-done(((bf16[1536,512]{1,0:T(8,128)(2,1)}), bf16[384,512]{1,0:T(8,128)(2,1)}) %reduce-scatter.35.cloned.1.call-update) | async-done | bytes 393232
  681.5 32.2 %reduce-scatter.27.cloned.1.call-done = bf16[512,512]{1,0:T(8,128)(2,1)} async-done(((bf16[512,2048]{1,0:T(8,128)(2,1)}), bf16[512,512]{1,0:T(8,128)(2,1)}) %reduce-scatter.27.cloned.1.call-update) | async-done | bytes 524304 | tf_op jit(solution)/shard_map/reduce_scatter | solution.py:304
  713.7 61.0 %reduce-scatter.29.cloned.1.call-done = bf16[3072,256]{1,0:T(8,128)(2,1)} async-done(((bf16[3072,1024]{1,0:T(8,128)(2,1)}), bf16[3072,256]{1,0:T(8,128)(2,1)}) %reduce-scatter.29.cloned.1.call-update) | async-done | bytes 1572880 | tf_op jit(solution)/shard_map/reduce_scatter | solution.py:316
  774.7 7.1 fusion.63
  790.5 6.2 reduce-scatter.41.cloned.1.call-done
  797.5 21.2 %reduce-scatter.43.cloned.1.call-done = bf16[128,3]{1,0:T(8,128)(2,1)} async-done(((bf16[512,3]{1,0:T(8,128)(2,1)}), bf16[128,3]{1,0:T(8,128)(2,1)}) %reduce-scatter.43.cloned.1.call-update) | async-done | bytes 784
  819.6 22.3 %reduce-scatter.45.cloned.1.call-done = bf16[256,3]{1,0:T(8,128)(2,1)} async-done(((bf16[1024,3]{1,0:T(8,128)(2,1)}), bf16[256,3]{1,0:T(8,128)(2,1)}) %reduce-scatter.45.cloned.1.call-update) | async-done | bytes 1552
  842.8 22.0 %all-reduce = (bf16[3,128]{1,0:T(4,128)(2,1)S(1)}, bf16[3,128]{1,0:T(4,128)(2,1)S(1)}, bf16[3,256]{1,0:T(4,128)(2,1)S(1)}) all-reduce(bf16[3,128]{1,0:T(4,128)(2,1)S(1)} %copy.107, bf16[3,128]{1,0:T(4,128)(2,1)S(1)} %copy.109, bf16[3,256]{1,0:T(4,128)(2,1)S(1)} %copy.111), channel_id=1, replica_groups=mesh['obj'=8,'blk'=4] {'obj'}, use_global_device_ids=true, to_apply=%region_38.39 | all-reduce | flops 1536 | bytes 6144 | tf_op jit(solution)/shard_map/psum | solution.py:333
  869.3 122.5 %all-reduce.7.cloned.1.call-done = (bf16[384,256]{0,1:T(8,128)(2,1)}, bf16[512,128]{1,0:T(8,128)(2,1)}, bf16[512,128]{1,0:T(8,128)(2,1)}, bf16[512,384]{1,0:T(8,...) async-done(((bf16[384,256]{0,1:T(8,128)(2,1)}, bf16[512,128]{1,0:T(8,128)(2,1)}, ...) | async-done | bytes 3604496 | tf_op jit(solution)/shard_map/psum | solution.py:337
  (440 shorter events, 232.1 us)
Async XLA Ops:
  7.2 197.9 %copy-start = (bf16[512,2048]{1,0:T(8,128)(2,1)S(1)}, bf16[512,2048]{1,0:T(8,128)(2,1)}, u32[]{:S(2)}) copy-start(bf16[512,2048]{1,0:T(8,128)(2,1)} %param.27) | copy-start | bytes 6291460
  7.2 97.6 %all-gather.2.cloned.1.call-start = ((), (), s32[]{:S(2)}) async-start(), calls=%async_computation.10 | async-start | bytes 7864320 | tf_op jit(solution)/shard_map/all_gather | solution.py:204
  8.8 38.9 %copy-start.12 = (bf16[1,768,512]{1,2,0:T(8,128)(2,1)}, bf16[1,768,512]{1,2,0:T(8,128)(2,1)S(1)}, u32[]{:S(2)}) copy-start(bf16[1,768,512]{1,2,0:T(8,128)(2,1)S(1)} %copy.74) | copy-start | bytes 2359300
  15.2 33.6 %copy-start.73 = (f32[1,512]{1,0:T(1,128)}, f32[1,512]{1,0:T(1,128)S(1)}, u32[]{:S(2)}) copy-start(f32[1,512]{1,0:T(1,128)S(1)} %get-tuple-element.213) | copy-start | bytes 6148
  15.2 208.7 %copy-start.71 = (f32[1,512]{1,0:T(1,128)}, f32[1,512]{1,0:T(1,128)S(1)}, u32[]{:S(2)}) copy-start(f32[1,512]{1,0:T(1,128)S(1)} %get-tuple-element.212) | copy-start | bytes 6148
  21.8 7.2 copy-start.32
  31.0 7.7 copy-start.39
  31.0 7.7 copy-start.60
  38.7 9.0 copy-start.61
  38.7 9.0 copy-start.43
  55.5 522.1 %reduce-scatter.37.cloned.1.call-start = ((), (), s32[]{:S(2)}) async-start(), calls=%async_computation.17 | async-start | bytes 655360
  172.8 28.8 %copy-start.42 = (bf16[512,512]{1,0:T(8,128)(2,1)S(1)}, bf16[512,512]{1,0:T(8,128)(2,1)}, u32[]{:S(2)}) copy-start(bf16[512,512]{1,0:T(8,128)(2,1)} %param.26) | copy-start | bytes 1572868
  204.0 20.0 %copy-start.65 = (f32[768]{0:T(1024)}, f32[768]{0:T(1024)S(1)}, u32[]{:S(2)}) copy-start(f32[768]{0:T(1024)S(1)} %broadcast_multiply_fusion.6) | copy-start | bytes 9220
  204.2 19.8 %copy-start.77 = (f32[768]{0:T(1024)}, f32[768]{0:T(1024)S(1)}, u32[]{:S(2)}) copy-start(f32[768]{0:T(1024)S(1)} %add_rsqrt_fusion) | copy-start | bytes 9220
  234.8 7.0 copy-start.2
  261.3 20.2 %collective-permute-start.1 = (bf16[1,768,1024]{1,2,0:T(8,128)(2,1)}, bf16[1,768,1024]{1,2,0:T(8,128)(2,1)}, u32[]{:S(2)}, u32[]{:S(2)}) collective-permute-start(bf16[1,768,1024]{1,2,0:T(8,128)(2,1)} %fusion.214), channel_id=1, source_target_pairs={{3,0},{0,1},{1,2},{2,3},{7,4},{4,5},{5,6},{6,7},{11,8},{8,9},{9,10... | collective-permute-start | bytes 4718600 | tf_op jit(solution)/shard_map/while/body/eval_jaxpr/ppermute | solution.py:18
  261.6 36.8 %collective-permute-start = (bf16[1,768,1024]{1,2,0:T(8,128)(2,1)}, bf16[1,768,1024]{1,2,0:T(8,128)(2,1)}, u32[]{:S(2)}, u32[]{:S(2)}) collective-permute-start(bf16[1,768,1024]{1,2,0:T(8,128)(2,1)} %copy.118), channel_id=1, source_target_pairs={{3,0},{0,1},{1,2},{2,3},{7,4},{4,5},{5,6},{6,7},{11,8},{8,9},{9,10... | collective-permute-start | bytes 4718600 | tf_op jit(solution)/shard_map/while/body/eval_jaxpr/ppermute | solution.py:18
  268.9 15.9 %copy-start.8 = (f32[1,768,512]{1,2,0:T(8,128)}, f32[1,768,512]{1,2,0:T(8,128)S(1)}, u32[]{:S(2)}) copy-start(f32[1,768,512]{1,2,0:T(8,128)S(1)} %bitcast_add_fusion.7) | copy-start | bytes 4718596 | tf_op jit(solution)/shard_map/while
  306.1 7.0 copy-start.2
  333.6 20.2 %collective-permute-start.1 = (bf16[1,768,1024]{1,2,0:T(8,128)(2,1)}, bf16[1,768,1024]{1,2,0:T(8,128)(2,1)}, u32[]{:S(2)}, u32[]{:S(2)}) collective-permute-start(bf16[1,768,1024]{1,2,0:T(8,128)(2,1)} %fusion.214), channel_id=1, source_target_pairs={{3,0},{0,1},{1,2},{2,3},{7,4},{4,5},{5,6},{6,7},{11,8},{8,9},{9,10... | collective-permute-start | bytes 4718600 | tf_op jit(solution)/shard_map/while/body/eval_jaxpr/ppermute | solution.py:18
  333.6 37.0 %collective-permute-start = (bf16[1,768,1024]{1,2,0:T(8,128)(2,1)}, bf16[1,768,1024]{1,2,0:T(8,128)(2,1)}, u32[]{:S(2)}, u32[]{:S(2)}) collective-permute-start(bf16[1,768,1024]{1,2,0:T(8,128)(2,1)} %copy.118), channel_id=1, source_target_pairs={{3,0},{0,1},{1,2},{2,3},{7,4},{4,5},{5,6},{6,7},{11,8},{8,9},{9,10... | collective-permute-start | bytes 4718600 | tf_op jit(solution)/shard_map/while/body/eval_jaxpr/ppermute | solution.py:18
  341.2 15.9 %copy-start.8 = (f32[1,768,512]{1,2,0:T(8,128)}, f32[1,768,512]{1,2,0:T(8,128)S(1)}, u32[]{:S(2)}) copy-start(f32[1,768,512]{1,2,0:T(8,128)S(1)} %bitcast_add_fusion.7) | copy-start | bytes 4718596 | tf_op jit(solution)/shard_map/while
  405.9 20.2 %collective-permute-start.1 = (bf16[1,768,1024]{1,2,0:T(8,128)(2,1)}, bf16[1,768,1024]{1,2,0:T(8,128)(2,1)}, u32[]{:S(2)}, u32[]{:S(2)}) collective-permute-start(bf16[1,768,1024]{1,2,0:T(8,128)(2,1)} %fusion.214), channel_id=1, source_target_pairs={{3,0},{0,1},{1,2},{2,3},{7,4},{4,5},{5,6},{6,7},{11,8},{8,9},{9,10... | collective-permute-start | bytes 4718600 | tf_op jit(solution)/shard_map/while/body/eval_jaxpr/ppermute | solution.py:18
  405.9 37.0 %collective-permute-start = (bf16[1,768,1024]{1,2,0:T(8,128)(2,1)}, bf16[1,768,1024]{1,2,0:T(8,128)(2,1)}, u32[]{:S(2)}, u32[]{:S(2)}) collective-permute-start(bf16[1,768,1024]{1,2,0:T(8,128)(2,1)} %copy.118), channel_id=1, source_target_pairs={{3,0},{0,1},{1,2},{2,3},{7,4},{4,5},{5,6},{6,7},{11,8},{8,9},{9,10... | collective-permute-start | bytes 4718600 | tf_op jit(solution)/shard_map/while/body/eval_jaxpr/ppermute | solution.py:18
  413.5 15.9 %copy-start.8 = (f32[1,768,512]{1,2,0:T(8,128)}, f32[1,768,512]{1,2,0:T(8,128)S(1)}, u32[]{:S(2)}) copy-start(f32[1,768,512]{1,2,0:T(8,128)S(1)} %bitcast_add_fusion.7) | copy-start | bytes 4718596 | tf_op jit(solution)/shard_map/while
  447.9 7.0 copy-start.4
  447.9 7.0 copy-start.38
  471.5 20.2 %collective-permute-start.2 = (bf16[1,768,1024]{1,2,0:T(8,128)(2,1)}, bf16[1,768,1024]{1,2,0:T(8,128)(2,1)}, u32[]{:S(2)}, u32[]{:S(2)}) collective-permute-start(bf16[1,768,1024]{1,2,0:T(8,128)(2,1)} %fusion.30), channel_id=1, source_target_pairs={{3,0},{0,1},{1,2},{2,3},{7,4},{4,5},{5,6},{6,7},{11,8},{8,9},{9,10... | collective-permute-start | bytes 4718600 | tf_op jit(solution)/shard_map/ppermute | solution.py:18
  473.9 110.1 %all-reduce.5.cloned.1.call-start = ((), (), s32[]{:S(2)}) async-start(), calls=%async_computation.11 | async-start | bytes 2621440 | tf_op jit(solution)/shard_map/psum | solution.py:277
  480.7 11.0 %copy-start.116 = (bf16[512,1536]{1,0:T(8,128)(2,1)S(1)}, bf16[512,1536]{1,0:T(8,128)(2,1)}, u32[]{:S(2)}) copy-start(bf16[512,1536]{1,0:T(8,128)(2,1)} %param.25) | copy-start | bytes 4718596
  480.9 15.5 %copy-start.51 = (bf16[1,768,512]{1,2,0:T(8,128)(2,1)}, bf16[1,768,512]{1,2,0:T(8,128)(2,1)S(1)}, u32[]{:S(2)}) copy-start(bf16[1,768,512]{1,2,0:T(8,128)(2,1)S(1)} %fusion.51) | copy-start | bytes 2359300
  507.3 9.4 copy-start.33
  507.3 15.0 %slice-start = ((s8[14352384]{0:T(1024)(128)(4,1)}), s8[1769472]{0:T(1024)(128)(4,1)S(1)}, s32[]{:S(2)}) async-start(s8[14352384]{0:T(1024)(128)(4,1)} %bitcast.371), calls=%async_computation.23 | async-start | bytes 3538944
  507.3 15.0 %slice-start.1 = ((s8[14352384]{0:T(1024)(128)(4,1)}), s8[4194304]{0:T(1024)(128)(4,1)S(1)}, s32[]{:S(2)}) async-start(s8[14352384]{0:T(1024)(128)(4,1)} %bitcast.371), calls=%async_computation.24 | async-start | bytes 8388608
  507.4 15.0 %slice-start.2 = ((s8[14352384]{0:T(1024)(128)(4,1)}), s8[4194304]{0:T(1024)(128)(4,1)S(1)}, s32[]{:S(2)}) async-start(s8[14352384]{0:T(1024)(128)(4,1)} %bitcast.371), calls=%async_computation.25 | async-start | bytes 8388608
  526.4 63.9 %reduce-scatter.31.cloned.1.call-start = ((), (), s32[]{:S(2)}) async-start(), calls=%async_computation.14 | async-start | bytes 655360
  533.7 81.2 %reduce-scatter.33.cloned.1.call-start = ((), (), s32[]{:S(2)}) async-start(), calls=%async_computation.15 | async-start | bytes 655360
  537.0 111.8 %reduce-scatter.39.cloned.1.call-start = ((), (), s32[]{:S(2)}) async-start(), calls=%async_computation.18 | async-start | bytes 2621440
  548.2 131.4 %reduce-scatter.35.cloned.1.call-start = ((), (), s32[]{:S(2)}) async-start(), calls=%async_computation.16 | async-start | bytes 1966080
  555.9 157.8 %reduce-scatter.27.cloned.1.call-start = ((), (), s32[]{:S(2)}) async-start(), calls=%async_computation.12 | async-start | bytes 2621440 | tf_op jit(solution)/shard_map/reduce_scatter | solution.py:304
  562.6 212.1 %reduce-scatter.29.cloned.1.call-start = ((), (), s32[]{:S(2)}) async-start(), calls=%async_computation.13 | async-start | bytes 7864320 | tf_op jit(solution)/shard_map/reduce_scatter | solution.py:316
  577.0 7.0 copy-start.47
  577.0 219.7 %reduce-scatter.41.cloned.1.call-start = ((), (), s32[]{:S(2)}) async-start(), calls=%async_computation.19 | async-start | bytes 163840
  582.0 236.7 %reduce-scatter.43.cloned.1.call-start = ((), (), s32[]{:S(2)}) async-start(), calls=%async_computation.20 | async-start | bytes 163840
  582.9 258.9 %reduce-scatter.45.cloned.1.call-start = ((), (), s32[]{:S(2)}) async-start(), calls=%async_computation.21 | async-start | bytes 327680
  583.9 407.9 %all-reduce.7.cloned.1.call-start = ((), (), s32[]{:S(2)}) async-start(), calls=%async_computation.22 | async-start | bytes 7208960 | tf_op jit(solution)/shard_map/psum | solution.py:337
  787.3 79.2 %copy-start.36 = (bf16[384,1024]{1,0:T(8,128)(2,1)S(1)}, bf16[384,1024]{1,0:T(8,128)(2,1)}, u32[]{:S(2)}) copy-start(bf16[384,1024]{1,0:T(8,128)(2,1)} %param.23) | copy-start | bytes 2359300
  787.3 79.2 %copy-start.45 = (bf16[1,581,1024]{1,2,0:T(8,128)(2,1)S(1)}, bf16[1,581,1024]{1,2,0:T(8,128)(2,1)}, u32[]{:S(2)}) copy-start(bf16[1,581,1024]{1,2,0:T(8,128)(2,1)} %all-reduce.5.cloned.1.call-done) | copy-start | bytes 3569668
  (103 other events, 306.0 us)
Sparse Core Ops, SparseCore 0:
  55.6 49.0 all-gather.1
  474.0 22.2 reduce-scatter.36
  526.4 38.9 all-reduce.4
  568.5 21.6 reduce-scatter.30
  593.1 21.6 reduce-scatter.32
  617.4 31.3 reduce-scatter.38
  651.4 28.1 reduce-scatter.34
  682.3 31.3 reduce-scatter.26
  716.3 58.3 reduce-scatter.28
  777.1 19.5 reduce-scatter.40
  799.1 19.5 reduce-scatter.42
  821.8 20.0 reduce-scatter.44
  847.5 144.2 all-reduce.6
where the time goes:
time: 1020 us; the launch traced here: 1010 us
  waiting for transfers between devices  484 us (47%)
  matrix products  269 us (26%)
  local copies, waits for them, and re-layouts  122 us (12%)
  other arithmetic  94.4 us (9%)
  blocking collectives  22 us (2%)
  between operations  16.1 us (2%)
    unnamed x21, waiting for transfers between devices  138 us
    psum x1, waiting for transfers between devices, body(): lax.psum(ckv_grad.astype(jnp.bfloat16), 'obj').astype(jnp.float32)  123 us
    ppermute x7, waiting for transfers between devices, from_behind(): return lax.ppermute(block, axis, route)  89 us
    reduce_scatter x1, waiting for transfers between devices, body(): lax.psum_scatter(modw_grad.reshape(3 * cam_width, 2 * D).astype(jnp.bfloa...  61 us
    unnamed x261, local copies, waits for them, and re-layouts  57.6 us
    dot_general x5, matrix products, attention_back(): jnp.einsum('oshd,okhd->ohsk', head_split(grad_out), head_split(value_rows...  47.2 us
    dot_general x6, matrix products, score_rows(): jnp.einsum('oshd,okhd->ohsk', head_split(queries), head_split(key_rows),...  46.6 us
    all_gather x1, waiting for transfers between devices, body(): lax.all_gather(own_pair, 'blk', axis=1, tiled=True)  40.8 us
  transfers between devices with their start and end apart: 20, of which 18 were waited for; matrix products, arithmetic and copies ran while one was open for 16% of the time, Pallas kernels for 0%

commit v1 on v0

v1 whole, which is shorter than its diff:
```python
import functools

import jax
import jax.numpy as jnp
from jax import lax
from jax.experimental import pallas as pl
from jax.experimental.pallas import tpu as pltpu
from jax.sharding import PartitionSpec as P

D = 512
HEADS = 8
HEAD_DIM = 64
PAIRS = HEADS // 2
WIDE = 2 * HEAD_DIM
LOG2E = 1.4426950408889634
LN2 = 0.6931471805599453
QUERY_FACTOR = LOG2E * HEAD_DIM ** (-0.5)
SCORE_FACTOR = HEAD_DIM ** (-0.5)
SAFE_SQUARE = 60.0 ** 2
EPSILON = 1e-06
GELU_A = 0.7978845608028654
GELU_B = 0.044715
MIB = 2**20

f32 = jnp.float32
bf16 = jnp.bfloat16
VMEM = pltpu.VMEM


def nn(a, b):
    return lax.dot_general(a, b, (((1,), (0,)), ((), ())), preferred_element_type=f32)


def nt(a, b):
    return lax.dot_general(a, b, (((1,), (1,)), ((), ())), preferred_element_type=f32)


def tn(a, b):
    return lax.dot_general(a, b, (((0,), (0,)), ((), ())), preferred_element_type=f32)


def whole():
    return pl.BlockSpec(memory_space=VMEM)


def params(mib=60):
    return pltpu.CompilerParams(vmem_limit_bytes=mib * MIB)


def lower_half(shape):
    return lax.broadcasted_iota(jnp.int32, shape, 1) % WIDE < HEAD_DIM


def own_half(shape, odd):
    lower = lower_half(shape)
    return jnp.logical_not(lower) if odd else lower


def normalize(x):
    center = x - jnp.mean(x, -1, keepdims=True)
    inverse = lax.rsqrt(jnp.mean(center * center, -1, keepdims=True) + EPSILON)
    return center * inverse, inverse


def modulate(x, gain, bias, shift, scale):
    normed, _ = normalize(x)
    return (normed * gain + bias) * (1.0 + scale) + shift


def modulate_back(g, x, gain, bias, scale):
    normed, inverse = normalize(x)
    affine = normed * gain + bias
    shift_grad = jnp.sum(g, 0, keepdims=True)
    scale_grad = jnp.sum(g * affine, 0, keepdims=True)
    a = g * (1.0 + scale)
    gain_grad = jnp.sum(a * normed, 0, keepdims=True)
    bias_grad = jnp.sum(a, 0, keepdims=True)
    n = a * gain
    back = inverse * (
        n - jnp.mean(n, -1, keepdims=True) - normed * jnp.mean(n * normed, -1, keepdims=True)
    )
    return back, jnp.concatenate([shift_grad, scale_grad, gain_grad, bias_grad], 0)


def norm_rows(gain_ref, bias_ref, mod_ref, j):
    gain = gain_ref[j : j + 1, :].astype(f32)
    bias = bias_ref[j : j + 1, :].astype(f32)
    shift = mod_ref[j : j + 1, :D]
    scale = mod_ref[j : j + 1, D:]
    return gain, bias, shift, scale


def head_sums(values, sign):
    rows = lax.broadcasted_iota(jnp.int32, (WIDE, WIDE), 0)
    cols = lax.broadcasted_iota(jnp.int32, (WIDE, WIDE), 1)
    block = jnp.where((rows < HEAD_DIM) != (cols < HEAD_DIM), sign, 0.0).astype(bf16)
    high = values.astype(bf16)
    low = (values - high.astype(f32)).astype(bf16)
    return nn(high, block) + nn(low, block)


def delta_lanes(product):
    parts = []
    for p in range(PAIRS):
        total = head_sums(product[:, p * WIDE : (p + 1) * WIDE], -1.0)
        high = total.astype(bf16).astype(f32)
        low = total - high
        lane = lax.broadcasted_iota(jnp.int32, total.shape, 1) % HEAD_DIM
        parts.append(jnp.where(lane == 0, high, jnp.where(lane == 1, low, 0.0)).astype(bf16))
    return jnp.concatenate(parts, 1)


def bounded(q, k):
    ok = None
    for p in range(PAIRS):
        cols = slice(p * WIDE, (p + 1) * WIDE)
        qp = q[:, cols].astype(f32)
        kp = k[:, cols].astype(f32)
        q_top = jnp.max(head_sums(qp * qp, 1.0))
        k_top = jnp.max(head_sums(kp * kp, 1.0))
        here = q_top * k_top < SAFE_SQUARE
        ok = here if ok is None else jnp.logical_and(ok, here)
    return ok


def attend_pair(safe, q_pair, k_pair, v_pair, w_ref, rows, real_keys):
    keys = k_pair.shape[0]
    count = q_pair.shape[0]
    outs = []
    for odd in (0, 1):
        own_k = own_half(k_pair.shape, odd)
        k_h = jnp.where(own_k, k_pair, jnp.zeros_like(k_pair))
        v_h = value_rows(v_pair, odd, real_keys)

        def blocks(shifted):
            parts = []
            for r in range(0, count, rows):
                s = nt(q_pair[r : r + rows], k_h)
                if shifted:
                    s = s - jnp.max(s, -1, keepdims=True)
                w = jnp.exp2(s).astype(bf16)
                w_ref[odd, r : r + rows, :] = w
                parts.append(nn(w, v_h))
            return jnp.concatenate(parts, 0)

        outs.append(lax.cond(safe, lambda: blocks(False), lambda: blocks(True)))
    lower = lower_half(outs[0].shape)
    merged = jnp.where(lower, outs[0], outs[1])
    sums = pltpu.roll(jnp.where(lower, outs[1], outs[0]), HEAD_DIM, 1)
    inverse = 1.0 / sums
    return merged * inverse, inverse


def value_rows(v_pair, odd, real_keys):
    own = own_half(v_pair.shape, odd)
    v_h = jnp.where(own, v_pair, jnp.ones_like(v_pair))
    if real_keys < v_pair.shape[0]:
        row = lax.broadcasted_iota(jnp.int32, v_pair.shape, 0)
        v_h = jnp.where(row < real_keys, v_h, jnp.zeros_like(v_h))
    return v_h


def attend_back_pair(do_pair, x_pair, do_t, q_t, k_pair, v_pair, w_of, chunk, real_keys, dkt_ref, dvt_ref):
    keys = k_pair.shape[0]
    dq = None
    for odd in (0, 1):
        own_q = own_half(do_pair.shape, odd)
        left = jnp.where(own_q, do_pair, x_pair)
        own_k = own_half(k_pair.shape, odd)
        k_h = jnp.where(own_k, k_pair, jnp.zeros_like(k_pair))
        v_h = value_rows(v_pair, odd, real_keys)
        head = slice(odd * HEAD_DIM, (odd + 1) * HEAD_DIM)
        for c in range(0, keys, chunk):
            cols = slice(c, c + chunk)
            w = w_of(odd, cols)
            dp = nt(left, v_h[cols])
            ds = (w.astype(f32) * dp).astype(bf16)
            part = nn(ds, k_h[cols])
            dq = part if dq is None else dq + part
            dkt_ref[head, cols] = (nn(q_t[head], ds) * LN2).astype(dkt_ref.dtype)
            dvt_ref[head, cols] = nn(do_t[head], w).astype(dvt_ref.dtype)
    return dq * SCORE_FACTOR


def cross_kernel(
    context_count, tokens, context, wq, wkv, wo, gain, bias, mod,
    second_in, after_one, q_out, pair_out, w_out, att_out, inv_out,
):
    x = tokens[...].astype(f32)
    first_in = modulate(x, *norm_rows(gain, bias, mod, 0)).astype(bf16)
    q = (nn(first_in, wq[...]) * QUERY_FACTOR).astype(bf16)
    pair = nn(context[...], wkv[...]).astype(bf16)
    q_out[...] = q
    pair_out[...] = pair
    safe = bounded(q, pair[:, :D])
    rows = min(256, q.shape[0])
    for p in range(PAIRS):
        cols = slice(p * WIDE, (p + 1) * WIDE)
        vcols = slice(D + p * WIDE, D + (p + 1) * WIDE)
        att, inverse = attend_pair(
            safe, q[:, cols], pair[:, cols], pair[:, vcols],
            w_out.at[2 * p : 2 * p + 2], rows, context_count,
        )
        att_out[:, cols] = att
        inv_out[:, cols] = inverse
    one = x + nn(att_out[...].astype(bf16), wo[...])
    after_one[...] = one
    second_in[...] = modulate(one, *norm_rows(gain, bias, mod, 1)).astype(bf16)


def self_kernel(own_in, all_in, wqkv, w_out, att_out, inv_out, q_out, kv_out, safe_ref):
    length = all_in.shape[0]
    g = pl.program_id(0)

    @pl.when(g == 0)
    def _():
        q_out[...] = (nn(own_in[...], wqkv[:, :D]) * QUERY_FACTOR).astype(bf16)
        step = 768 if length % 768 == 0 else length
        for r in range(0, length, step):
            kv_out[r : r + step, :] = nn(all_in[r : r + step, :], wqkv[:, D:]).astype(bf16)
        ok = bounded(q_out[...], kv_out[:, :D])
        safe_ref[0] = ok.astype(jnp.int32)

    cols = pl.ds(pl.multiple_of(g * WIDE, WIDE), WIDE)
    vcols = pl.ds(pl.multiple_of(D + g * WIDE, WIDE), WIDE)
    att, inverse = attend_pair(
        safe_ref[0] == 1, q_out[:, cols], kv_out[:, cols], kv_out[:, vcols],
        w_out, min(256, own_in.shape[0]), length,
    )
    att_out[:, cols] = att
    inv_out[:, cols] = inverse


def slabs(out_ref, base, grad):
    parts = out_ref.shape[0]
    rows, columns = grad.shape
    each = columns // parts
    lanes = out_ref.shape[2]
    for b in range(parts):
        for i in range(each // lanes):
            start = b * each + i * lanes
            out_ref[b, base + i * rows : base + (i + 1) * rows, :] = grad[
                :, start : start + lanes
            ].astype(out_ref.dtype)


def mlp_kernel(
    self_att, after_one, inv, cotangent, wo, up, down, gain, bias, mod,
    mixed, grad_two, do_out, x_out, modes, g_out,
):
    self_low = self_att[...].astype(bf16)
    two = after_one[...] + nn(self_low, wo[...])
    rows3 = norm_rows(gain, bias, mod, 2)
    third_in = modulate(two, *rows3).astype(bf16)
    cot = cotangent[...]
    final = two
    norm_grad = jnp.zeros_like(two)
    ff = up.shape[1]
    step = 512
    up_base = D * (D // g_out.shape[0] // g_out.shape[2])
    for f in range(0, ff, step):
        hidden = nn(third_in, up[:, f : f + step])
        square = hidden * hidden
        inner = GELU_A * hidden * (1.0 + GELU_B * square)
        t = jnp.tanh(inner)
        half = 0.5 * (1.0 + t)
        active = (hidden * half).astype(bf16)
        slope = half + 0.5 * hidden * (1.0 - t * t) * (GELU_A * (1.0 + 3.0 * GELU_B * square))
        final = final + nn(active, down[f : f + step, :])
        hidden_grad = (nt(cot, down[f : f + step, :]) * slope).astype(bf16)
        norm_grad = norm_grad + nt(hidden_grad, up[:, f : f + step])
        up_part = tn(third_in, hidden_grad)
        down_part = tn(active, cot)
        parts, _, lanes = g_out.shape
        each = ff // parts
        for i in range(step // lanes):
            col = f + i * lanes
            b, inside = col // each, col % each // lanes
            base = up_base + inside * D
            g_out[b, base : base + D, :] = up_part[:, i * lanes : (i + 1) * lanes].astype(bf16)
        down_base = up_base + D * (each // lanes)
        for b in range(parts):
            for i in range(D // parts // lanes):
                start = b * (D // parts) + i * lanes
                base = down_base + i * ff + f
                g_out[b, base : base + step, :] = down_part[:, start : start + lanes].astype(bf16)
    mixed[...] = final.astype(bf16)
    back, sums = modulate_back(norm_grad, two, rows3[0], rows3[1], rows3[3])
    modes[...] = sums
    grad = cot.astype(f32) + back
    grad_two[...] = grad
    self_grad = grad.astype(bf16)
    slabs(g_out, 0, tn(self_low, self_grad))
    do = (nt(self_grad, wo[...]) * inv[...]).astype(bf16)
    do_out[...] = do
    x_out[...] = delta_lanes(do.astype(f32) * self_att[...])


def self_back_kernel(do, x, q, kv, w, dq_out, dkvt_out, do_t, q_t):
    g = pl.program_id(0)

    @pl.when(g == 0)
    def _():
        do_t[...] = do[...].T
        q_t[...] = q[...].T

    length = kv.shape[0]
    cols = pl.ds(pl.multiple_of(g * WIDE, WIDE), WIDE)
    vcols = pl.ds(pl.multiple_of(D + g * WIDE, WIDE), WIDE)
    dq = attend_back_pair(
        do[:, cols], x[:, cols], do_t[cols, :], q_t[cols, :], kv[:, cols], kv[:, vcols],
        lambda odd, c: w[odd, :, c], 512, length, dkvt_out.at[cols, :], dkvt_out.at[vcols, :],
    )
    dq_out[:, cols] = dq.astype(bf16)


def joint_back_kernel(all_in, own_in, dq, dkvt, wqkv, part_out, own_part, g_out):
    length = all_in.shape[0]
    step = 512
    for c in range(0, length, step):
        part_out[c : c + step, :] = tn(dkvt[:, c : c + step], wqkv_t(wqkv)).astype(bf16)
    own_part[...] = nt(dq[...], wqkv[:, :D])
    grad_q = tn(own_in[...], dq[...])
    grad_kv = nn(dkvt[...], all_in[...]).T
    slabs(g_out, 0, jnp.concatenate([grad_q, grad_kv], 1))


def wqkv_t(wqkv):
    return wqkv[:, D:].T


def cross_back_kernel(
    context_count, norm_part, own_part, grad_two, after_one, tokens, context, q, pair, w, att, inv,
    wq, wkv, wo, gain, bias, mod,
    tokens_grad, context_out, modes, g_out, dkvt,
):
    rows2 = norm_rows(gain, bias, mod, 1)
    back, sums_two = modulate_back(
        norm_part[...].astype(f32) + own_part[...], after_one[...], rows2[0], rows2[1], rows2[3]
    )
    grad_one = grad_two[...] + back
    cross_grad = grad_one.astype(bf16)
    out_rows = D * (D // g_out.shape[0] // g_out.shape[2])
    slabs(g_out, 0, tn(att[...].astype(bf16), cross_grad))
    do = (nt(cross_grad, wo[...]) * inv[...]).astype(bf16)
    x = delta_lanes(do.astype(f32) * att[...])
    do_t = do.T
    q_t = q[...].T
    parts = []
    for p in range(PAIRS):
        cols = slice(p * WIDE, (p + 1) * WIDE)
        vcols = slice(D + p * WIDE, D + (p + 1) * WIDE)
        dq = attend_back_pair(
            do[:, cols], x[:, cols], do_t[cols, :], q_t[cols, :], pair[:, cols], pair[:, vcols],
            lambda odd, c, p=p: w[2 * p + odd, :, c], pair.shape[0], context_count,
            dkvt.at[cols, :], dkvt.at[vcols, :],
        )
        parts.append(dq.astype(bf16))
    dq = jnp.concatenate(parts, 1)
    first = tokens[...].astype(f32)
    rows1 = norm_rows(gain, bias, mod, 0)
    first_in = modulate(first, *rows1).astype(bf16)
    slabs(g_out, out_rows, tn(first_in, dq))
    back, sums_one = modulate_back(nt(dq, wq[...]), first, rows1[0], rows1[1], rows1[3])
    tokens_grad[...] = grad_one + back
    modes[...] = jnp.concatenate([sums_one, sums_two], 0)
    real = lax.broadcasted_iota(jnp.int32, dkvt.shape, 1) < context_count
    kept = jnp.where(real, dkvt[...], jnp.zeros_like(dkvt))
    slabs(g_out, 2 * out_rows, nn(kept, context[...]).T)
    context_out[...] = tn(dkvt[...], wkv[...].T).astype(bf16)


def shape(dims, dtype):
    return jax.ShapeDtypeStruct(tuple(dims), dtype)


def body(
    tokens, context, camera_groups, camera_table, cross_query, cross_kv, cross_out, self_qkv,
    self_out, mlp_up, mlp_down, norm_gain, norm_bias, mod_weight, mod_bias, cotangent,
):
    parts = lax.axis_size("blk")
    tokens = tokens[0]
    cotangent = cotangent[0]
    context_count = context.shape[1]
    rows = tokens.shape[0]
    length = rows * parts
    ff = mlp_up.shape[1]
    cam_width = mod_weight.shape[1]
    ctx_width = context.shape[2]
    padded = -(-context_count // 128) * 128
    context_rows = jnp.pad(context[0], ((0, padded - context_count), (0, 0)), mode="edge")

    picked = (
        camera_groups[:, None] == jnp.arange(camera_table.shape[0], dtype=jnp.int32)[None, :]
    ).astype(bf16)
    camera = jnp.dot(picked, camera_table, preferred_element_type=f32)
    lifted = jax.nn.silu(camera).astype(bf16)
    mod = (
        jnp.einsum("oc,jcm->ojm", lifted, mod_weight, preferred_element_type=f32)
        + mod_bias.astype(f32)
    )[0]

    second_in, after_one, cross_q, cross_pair, cross_w, cross_att, cross_inv = pl.pallas_call(
        functools.partial(cross_kernel, context_count),
        out_shape=[
            shape((rows, D), bf16), shape((rows, D), f32), shape((rows, D), bf16),
            shape((padded, 2 * D), bf16), shape((HEADS, rows, padded), bf16),
            shape((rows, D), f32), shape((rows, D), f32),
        ],
        in_specs=[whole()] * 8,
        out_specs=[whole()] * 7,
        compiler_params=params(),
        name="cross_forward",
    )(tokens, context_rows, cross_query, cross_kv, cross_out, norm_gain, norm_bias, mod)

    all_in = lax.all_gather(second_in, "blk", axis=0, tiled=True)

    full = lambda *dims: pl.BlockSpec(dims, lambda g: (0,) * len(dims))
    self_w, self_att, self_inv, self_q, self_kv = pl.pallas_call(
        self_kernel,
        grid=(PAIRS,),
        out_shape=[
            shape((HEADS, rows, length), bf16), shape((rows, D), f32), shape((rows, D), f32),
            shape((rows, D), bf16), shape((length, 2 * D), bf16),
        ],
        in_specs=[full(rows, D), full(length, D), full(D, 3 * D)],
        out_specs=[
            pl.BlockSpec((2, rows, length), lambda g: (g, 0, 0)),
            full(rows, D), full(rows, D), full(rows, D), full(length, 2 * D),
        ],
        scratch_shapes=[pltpu.SMEM((1,), jnp.int32)],
        compiler_params=params(),
        name="self_forward",
    )(second_in, all_in, self_qkv)

    each = D // parts
    lanes = min(128, each)
    tall = lambda columns, depth: depth * (columns // parts // lanes)
    early = tall(D, D) + tall(ff, D) + tall(D, ff)
    mixed, grad_two, self_do, self_x, modes_three, g_early = pl.pallas_call(
        mlp_kernel,
        out_shape=[
            shape((rows, D), bf16), shape((rows, D), f32), shape((rows, D), bf16),
            shape((rows, D), bf16), shape((4, D), f32), shape((parts, early, lanes), bf16),
        ],
        in_specs=[whole()] * 10,
        out_specs=[whole()] * 6,
        compiler_params=params(),
        name="feed_forward",
    )(self_att, after_one, self_inv, cotangent, self_out, mlp_up, mlp_down, norm_gain, norm_bias, mod)

    dq, dkvt = pl.pallas_call(
        self_back_kernel,
        grid=(PAIRS,),
        out_shape=[shape((rows, D), bf16), shape((2 * D, length), bf16)],
        in_specs=[
            full(rows, D), full(rows, D), full(rows, D), full(length, 2 * D),
            pl.BlockSpec((2, rows, length), lambda g: (g, 0, 0)),
        ],
        out_specs=[full(rows, D), full(2 * D, length)],
        scratch_shapes=[VMEM((D, rows), bf16), VMEM((D, rows), bf16)],
        compiler_params=params(),
        name="self_backward",
    )(self_do, self_x, self_q, self_kv, self_w)

    middle = tall(3 * D, D)
    norm_parts, own_part, g_middle = pl.pallas_call(
        joint_back_kernel,
        out_shape=[
            shape((length, D), bf16), shape((rows, D), f32), shape((parts, middle, lanes), bf16),
        ],
        in_specs=[whole()] * 5,
        out_specs=[whole()] * 3,
        compiler_params=params(),
        name="joint_backward",
    )(all_in, second_in, dq, dkvt, self_qkv)

    norm_part = lax.psum_scatter(norm_parts, "blk", scatter_dimension=0, tiled=True)

    late = 2 * tall(D, D) + tall(2 * D, ctx_width)
    tokens_grad, context_part, modes_low, g_late = pl.pallas_call(
        functools.partial(cross_back_kernel, context_count),
        out_shape=[
            shape((rows, D), f32), shape((padded, ctx_width), bf16), shape((8, D), f32),
            shape((parts, late, lanes), bf16),
        ],
        in_specs=[whole()] * 17,
        out_specs=[whole()] * 4,
        scratch_shapes=[VMEM((2 * D, padded), bf16)],
        compiler_params=params(),
        name="cross_backward",
    )(
        norm_part, own_part, grad_two, after_one, tokens, context_rows, cross_q, cross_pair, cross_w,
        cross_att, cross_inv, cross_query, cross_kv, cross_out, norm_gain, norm_bias, mod,
    )

    def reduced(g):
        part = lax.psum_scatter(g, "blk", scatter_dimension=0, tiled=True)
        return lax.psum(part, "obj")[0]

    early_sum = reduced(g_early)
    middle_sum = reduced(g_middle)
    late_sum = reduced(g_late)
    context_grad = lax.psum(context_part, "blk").astype(f32)[:context_count]

    def unslab(total, base, columns, depth):
        count = columns // parts // lanes
        pieces = [total[base + i * depth : base + (i + 1) * depth] for i in range(count)]
        return jnp.concatenate(pieces, 1).astype(f32)

    so = tall(D, D)
    self_out_grad = unslab(early_sum, 0, D, D)
    mlp_up_grad = unslab(early_sum, so, ff, D)
    mlp_down_grad = unslab(early_sum, so + tall(ff, D), D, ff)
    self_qkv_grad = unslab(middle_sum, 0, 3 * D, D)
    cross_out_grad = unslab(late_sum, 0, D, D)
    cross_query_grad = unslab(late_sum, so, D, D)
    cross_kv_grad = unslab(late_sum, 2 * so, 2 * D, ctx_width)

    small = jnp.concatenate([modes_low, modes_three], 0).reshape(3, 4, D)
    object_sums = lax.psum(small, "blk")
    everywhere = lax.all_gather(object_sums, "obj")
    lifted_all = lax.all_gather(lifted[0], "obj").astype(f32)
    mode_all = everywhere[:, :, :2].reshape(-1, 3, 2 * D)
    place = lax.axis_index("blk")
    width = 2 * D // parts
    mode_here = lax.dynamic_slice_in_dim(mode_all, place * width, width, 2)
    mod_weight_grad = jnp.einsum(
        "oc,ojm->jcm", lifted_all, mode_here, precision=lax.Precision.HIGHEST
    )
    mod_bias_grad = jnp.sum(mode_here, 0)
    norms = lax.dynamic_slice_in_dim(jnp.sum(everywhere[:, :, 2:], 0), place * each, each, 2)
    return (
        mixed[None], tokens_grad[None], context_grad[None], cross_query_grad, cross_kv_grad,
        cross_out_grad, self_qkv_grad, self_out_grad, mlp_up_grad, mlp_down_grad,
        norms[:, 0], norms[:, 1], mod_weight_grad, mod_bias_grad,
    )


def solution(mesh):
    rows = P("obj", "blk", None)
    columns = P(None, "blk")
    return jax.shard_map(
        body,
        mesh=mesh,
        in_specs=(rows, P("obj", None, None), P("obj")) + (P(),) * 12 + (rows,),
        out_specs=(rows, rows, P("obj", None, None)) + (columns,) * 9
        + (P(None, None, "blk"), columns),
        check_vma=False,
    )
```

time: 1020 us -> 516 us (0.51)
  matrix products: 269 us -> 5.33 us
  waiting for transfers between devices: 484 us -> 230 us
  Pallas kernels: 0 us -> 171 us
  local copies, waits for them, and re-layouts: 122 us -> 6.72 us
  other arithmetic: 94.4 us -> 10.2 us
  blocking collectives: 22 us -> 68.5 us
    dot_general x51 -> x3, matrix products: 269 us -> 5.33 us  [the longest x1 3.77 us: body(): jnp.einsum('oc,jcm->ojm', lifted, mod_weight, preferred_element_type=f32)]
    pallas_call x0 -> x6, Pallas kernels: none -> 171 us  [the longest x1 53 us: body(): pl.pallas_call(self_kernel, grid=(PAIRS,), out_shape=[shape((HEADS, rows,...]
    unnamed x21 -> x7, waiting for transfers between devices: 138 us -> 1.79 us
    ppermute x7 -> x0, waiting for transfers between devices: 89 us -> none  [from_behind(): return lax.ppermute(block, axis, route)]
    all_gather x0 -> x2, blocking collectives: none -> 58 us  [the longest x1 31.9 us: body(): everywhere = lax.all_gather(object_sums, 'obj')]
    psum x2, waiting for transfers between devices: 123 us -> 65.9 us  [the longest x1 65.9 us: reduced(): return lax.psum(part, 'obj')[0]]
    unnamed x261 -> x17, local copies, waits for them, and re-layouts: 57.6 us -> 4.84 us
    reduce_sum x14 -> x1, other arithmetic: 44.7 us -> 0.61 us  [body(): mod_bias_grad = jnp.sum(mode_here, 0)]
  transfers between devices with their start and end apart: 20 -> 7, of which waited for: 18 -> 6; matrix products, arithmetic and copies ran while one was open for 16% -> 2% of each run, Pallas kernels for 0% -> 4%
where the time goes in v1:
time: 516 us; the launch traced here: 508 us
  waiting for transfers between devices  230 us (45%)
  Pallas kernels  171 us (33%)
  blocking collectives  68.5 us (13%)
  between operations  15.3 us (3%)
  other arithmetic  10.2 us (2%)
  local copies, waits for them, and re-layouts  6.72 us (1%)
  matrix products  5.33 us (1%)
    reduce_scatter x3, waiting for transfers between devices, reduced(): part = lax.psum_scatter(g, 'blk', scatter_dimension=0, tiled=True)  91.7 us
    psum x1, waiting for transfers between devices, reduced(): return lax.psum(part, 'obj')[0]  65.9 us
    pallas_call x1, Pallas kernels, body(): pl.pallas_call(self_kernel, grid=(PAIRS,), out_shape=[shape((HEADS, rows,...  53 us
    pallas_call x1, Pallas kernels, body(): pl.pallas_call(self_back_kernel, grid=(PAIRS,), out_shape=[shape((rows, D...  43.6 us
    reduce_scatter x1, waiting for transfers between devices, body(): lax.psum_scatter(norm_parts, 'blk', scatter_dimension=0, tiled=True)  36.5 us
    all_gather x1, waiting for transfers between devices, body(): all_in = lax.all_gather(second_in, 'blk', axis=0, tiled=True)  34.2 us
    all_gather x1, blocking collectives, body(): everywhere = lax.all_gather(object_sums, 'obj')  31.9 us
    all_gather x1, blocking collectives, body(): lifted_all = lax.all_gather(lifted[0], 'obj').astype(f32)  26.1 us
  transfers between devices with their start and end apart: 7, of which 6 were waited for; matrix products, arithmetic and copies ran while one was open for 2% of the time, Pallas kernels for 4%

profile of v1, /device:TPU:0, one launch (start us, length us, event | category | flops | bytes accessed | tf_op | source)
XLA Modules:
  0.0 507.6 jit_solution(1910856596788465842)
XLA Ops:
  7.2 0.0 all-gather.3.cloned.1.call-start
  7.9 0.0 copy-done
  7.9 0.1 fusion.6
  8.0 0.7 slice_reduce_fusion.1
  8.8 3.8 fusion.13
  12.6 0.6 bitcast_add_fusion.mod
  13.2 0.9 pad_maximum_fusion.context
  14.0 18.3 %cross_forward.1 = (bf16[768,512]{1,0:T(8,128)(2,1)}, f32[768,512]{1,0:T(8,128)}, bf16[768,512]{1,0:T(8,128)(2,1)}, bf16[640,1024]{1,0:T(8,128)(2,1)}, bf16[8,76...) custom-call(bf16[768,512]{1,0:T(8,128)(2,1)} %bitcast.67, bf16[640,384]{1,0:T(8,128)(2,1)} %pad_maximum_fusion.context, ...), custom_call_target="tpu_custom_call" | custom-call | tf_op jit(solution)/shard_map/cross_forward/pallas_call | solution.py:403
  32.3 0.0 all-gather.3.cloned.1.call-update
  32.4 0.0 reduce-scatter.5.cloned.1.call-start
  32.4 34.2 %all-gather.3.cloned.1.call-done.all_in = bf16[3072,512]{1,0:T(8,128)(2,1)} async-done(((bf16[768,512]{1,0:T(8,128)(2,1)}), bf16[3072,512]{1,0:T(8,128)(2,1)}) %all-gather.3.cloned.1.call-update) | async-done | bytes 3145744 | tf_op jit(solution)/shard_map/all_gather | solution.py:416
  66.6 53.0 %self_forward.1 = (bf16[8,768,3072]{2,1,0:T(8,128)(2,1)}, f32[768,512]{1,0:T(8,128)}, f32[768,512]{1,0:T(8,128)}, bf16[768,512]{1,0:T(8,128)(2,1)}, bf16[3072,1024]{1,0:T(8,128)(2,1)}) custom-call(bf16[768,512]{1,0:T(8,128)(2,1)} %get-tuple-element.41.own_in, bf16[3072,512]{1,0:T(8,128)(2,1)} %all-gather.3.cloned.1.call-done.all_in, bf16[512,1536]{1,0:T(8,128)(2,1)} %wqkv.3), custom_call_target="tpu_custom_call" | custom-call | tf_op jit(solution)/shard_map/self_forward/pallas_call | solution.py:419
  119.6 20.8 %feed_forward.1 = (bf16[768,512]{1,0:T(8,128)(2,1)}, f32[768,512]{1,0:T(8,128)}, bf16[768,512]{1,0:T(8,128)(2,1)}, bf16[768,512]{1,0:T(8,128)(2,1)}, f32[4,512]{1,0:T(4,128)}, /*index=5*/bf16[4,4608,128]{2,1,0:T(8,128)(2,1)}) custom-call(f32[768,512]{1,0:T(8,128)} %get-tuple-element.42.self_att, f32[768,512]{1,0:T(8,128)} %get-tuple-element.43.after_one, ...), custom_call_target="tpu_custom_call" | custom-call | tf_op jit(solution)/shard_map/feed_forward/pallas_call | solution.py:440
  140.4 43.6 %self_backward.1 = (bf16[768,512]{1,0:T(8,128)(2,1)}, bf16[1024,3072]{1,0:T(8,128)(2,1)}) custom-call(bf16[768,512]{1,0:T(8,128)(2,1)} %get-tuple-element.46.do, bf16[768,512]{1,0:T(8,128)(2,1)} %get-tuple-element.47.x, bf16[768,512]{1,0:T(8,128)(2,1)} %get-tuple-element.48.q, bf16[3072,1024]{1,0:T(8,128)(2,1)} %get-tuple-element.49.kv, ...), custom_call_target="tpu_custom_call" | custom-call | tf_op jit(solution)/shard_map/self_backward/pallas_call | solution.py:452
  184.0 13.3 %joint_backward.1 = (bf16[3072,512]{1,0:T(8,128)(2,1)}, f32[768,512]{1,0:T(8,128)}, bf16[4,1536,128]{2,1,0:T(8,128)(2,1)}) custom-call(bf16[3072,512]{1,0:T(8,128)(2,1)} %all-gather.3.cloned.1.call-done.all_in, bf16[768,512]{1,0:T(8,128)(2,1)} %get-tuple-element.41.own_in, bf16[768,512]{1,0:T(8,128)(2,1)} %get-tuple-element.51.dq, ...), custom_call_target="tpu_custom_call" | custom-call | tf_op jit(solution)/shard_map/joint_backward/pallas_call | solution.py:467
  197.3 0.0 reduce-scatter.5.cloned.1.call-update
  197.4 0.0 reduce-scatter.9.cloned.1.call-start
  197.4 0.7 reduce-scatter.9.cloned.1.call-update
  198.1 0.0 reduce-scatter.11.cloned.1.call-start
  198.1 0.5 reduce-scatter.11.cloned.1.call-update
  198.7 0.3 reduce-scatter.7.cloned.1.call-start
  198.9 36.5 %reduce-scatter.5.cloned.1.call-done.norm_part = bf16[768,512]{1,0:T(8,128)(2,1)} async-done(((bf16[3072,512]{1,0:T(8,128)(2,1)}), bf16[768,512]{1,0:T(8,128)(2,1)}) %reduce-scatter.5.cloned.1.call-update) | async-done | bytes 786448 | tf_op jit(solution)/shard_map/reduce_scatter | solution.py:478
  235.5 21.8 %cross_backward.1 = (f32[768,512]{1,0:T(8,128)}, bf16[640,384]{1,0:T(8,128)(2,1)}, f32[8,512]{1,0:T(8,128)}, bf16[4,1792,128]{2,1,0:T(8,128)(2,1)}) custom-call(bf16[768,512]{1,0:T(8,128)(2,1)} %reduce-scatter.5.cloned.1.call-done.norm_part, f32[768,512]{1,0:T(8,128)} %get-tuple-element.54.own_part, f32[768,512]{1,0:T(8,128)} %get-tuple-element.55.grad_two, ...), custom_call_target="tpu_custom_call" | custom-call | tf_op jit(solution)/shard_map/cross_backward/pallas_call | solution.py:481
  257.3 0.0 reduce-scatter.7.cloned.1.call-update
  257.3 0.0 all-reduce.4.cloned.1.call-start
  257.4 0.5 all-reduce.4.cloned.1.call-update
  257.9 0.0 all-reduce.6.cloned.1.call-start
  257.9 8.5 %reduce-scatter.9.cloned.1.call-done = bf16[1,1536,128]{2,1,0:T(8,128)(2,1)} async-done(((bf16[4,1536,128]{2,1,0:T(8,128)(2,1)}), bf16[1,1536,128]{2,1,0:T(8,128)(2,1)}) %reduce-scatter.9.cloned.1.call-update) | async-done | bytes 393232 | tf_op jit(solution)/shard_map/reduce_scatter | solution.py:498
  266.4 50.3 %reduce-scatter.11.cloned.1.call-done = bf16[1,4608,128]{2,1,0:T(8,128)(2,1)} async-done(((bf16[4,4608,128]{2,1,0:T(8,128)(2,1)}), bf16[1,4608,128]{2,1,0:T(8,128)(2,1)}) %reduce-scatter.11.cloned.1.call-update) | async-done | bytes 1179664 | tf_op jit(solution)/shard_map/reduce_scatter | solution.py:498
  316.7 33.0 %reduce-scatter.7.cloned.1.call-done = bf16[1,1792,128]{2,1,0:T(8,128)(2,1)} async-done(((bf16[4,1792,128]{2,1,0:T(8,128)(2,1)}), bf16[1,1792,128]{2,1,0:T(8,128)(2,1)}) %reduce-scatter.7.cloned.1.call-update) | async-done | bytes 458768 | tf_op jit(solution)/shard_map/reduce_scatter | solution.py:498
  349.7 26.1 %all-gather = bf16[8192]{0:T(1024)(128)(2,1)S(1)} all-gather(bf16[1024]{0:T(1024)(128)(2,1)S(1)} %multiply_convert_fusion), channel_id=2, replica_groups=mesh['obj'=8,'blk'=4] {'obj'}, dimensions={0}, use_global_device_ids=true | all-gather | bytes 18432 | tf_op jit(solution)/shard_map/all_gather | solution.py:523
  375.8 10.5 %psum.39 = f32[1,3,4,512]{3,2,1,0:T(4,128)S(1)} all-reduce(f32[1,3,4,512]{3,2,1,0:T(4,128)S(1)} %all_gather.13), channel_id=1, replica_groups=mesh['obj'=8,'blk'=4] {'blk'}, use_global_device_ids=true, to_apply=%region_8.9 | all-reduce | flops 6144 | bytes 49152 | tf_op jit(solution)/shard_map/psum | solution.py:521
  386.4 31.9 %all_gather.14 = f32[8,3,4,512]{3,2,1,0:T(4,128)S(1)} all-gather(f32[1,3,4,512]{3,2,1,0:T(4,128)S(1)} %psum.39), channel_id=1, replica_groups=mesh['obj'=8,'blk'=4] {'obj'}, dimensions={0}, use_global_device_ids=true | all-gather | bytes 221184 | tf_op jit(solution)/shard_map/all_gather | solution.py:522
  418.3 0.1 fusion.12
  418.4 1.4 convolution_bitcast_fusion
  419.8 2.4 copy.35
  422.2 0.6 dynamic-slice_reduce_fusion
  422.8 0.1 constant_dynamic-slice_fusion.1
  422.9 0.6 copy_bitcast_fusion
  423.5 1.1 fusion.1
  424.6 1.8 copy.34
  426.4 65.9 %all-reduce.6.cloned.1.call-done = (bf16[1,1792,128]{2,1,0:T(8,128)(2,1)}, bf16[1,1536,128]{2,1,0:T(8,128)(2,1)}, bf16[1,4608,128]{2,1,0:T(8,128)(2,1)}) async-done(((bf16[1,1792,128]{2,1,0:T(8,128)(2,1)}, bf16[1,1536,128]{2,1,0:T(8,128)(2,1)}, bf16[1,4608,128]{2,1,0:T(8,128)(2,1)}), (bf16[1,1792,128]{2,1,0:T(8,128)(2,1)}, bf16[1,1536,128]{2,1,0:T(8,128)(2,1)}, ...) | async-done | bytes 2031632 | tf_op jit(solution)/shard_map/psum | solution.py:499
  492.3 1.0 slice_bitcast_fusion.13
  493.3 2.1 slice_bitcast_fusion.5
  495.5 2.1 fusion
  497.6 0.8 maximum_convert_fusion.2
  498.4 0.9 maximum_convert_fusion.1
  499.3 1.0 maximum_convert_fusion
  (23 shorter events, 0.2 us)
Async XLA Ops:
  7.2 0.7 copy-start
  7.2 59.4 %all-gather.3.cloned.1.call-start = ((), (), s32[]{:S(2)}) async-start(), calls=%async_computation.4 | async-start | bytes 3932160 | tf_op jit(solution)/shard_map/all_gather | solution.py:416
  8.8 3.8 copy-start.6
  8.8 4.4 copy-start.2
  32.4 203.1 %reduce-scatter.5.cloned.1.call-start = ((), (), s32[]{:S(2)}) async-start(), calls=%async_computation.5 | async-start | bytes 3932160 | tf_op jit(solution)/shard_map/reduce_scatter | solution.py:478
  197.4 69.1 %reduce-scatter.9.cloned.1.call-start = ((), (), s32[]{:S(2)}) async-start(), calls=%async_computation.8 | async-start | bytes 1966080 | tf_op jit(solution)/shard_map/reduce_scatter | solution.py:498
  198.1 118.6 %reduce-scatter.11.cloned.1.call-start = ((), (), s32[]{:S(2)}) async-start(), calls=%async_computation.9 | async-start | bytes 5898240 | tf_op jit(solution)/shard_map/reduce_scatter | solution.py:498
  198.7 151.0 %reduce-scatter.7.cloned.1.call-start = ((), (), s32[]{:S(2)}) async-start(), calls=%async_computation.7 | async-start | bytes 2293760 | tf_op jit(solution)/shard_map/reduce_scatter | solution.py:498
  257.3 118.5 %copy-start.4 = (f32[8,512]{1,0:T(8,128)S(1)}, f32[8,512]{1,0:T(8,128)}, u32[]{:S(2)}) copy-start(f32[8,512]{1,0:T(8,128)} %get-tuple-element.66) | copy-start | bytes 49156
  257.3 118.5 %copy-start.5 = (f32[4,512]{1,0:T(4,128)S(1)}, f32[4,512]{1,0:T(4,128)}, u32[]{:S(2)}) copy-start(f32[4,512]{1,0:T(4,128)} %get-tuple-element.67) | copy-start | bytes 24580
  257.3 166.2 %all-reduce.4.cloned.1.call-start = ((), (), s32[]{:S(2)}) async-start(), calls=%async_computation.6 | async-start | bytes 983040 | tf_op jit(solution)/shard_map/psum | solution.py:504
  257.9 234.4 %all-reduce.6.cloned.1.call-start = ((), (), s32[]{:S(2)}) async-start(), calls=%async_computation.10 | async-start | bytes 4063232 | tf_op jit(solution)/shard_map/psum | solution.py:499
  492.3 5.3 %copy-start.3 = (bf16[1,1536,128]{2,1,0:T(8,128)(2,1)S(1)}, bf16[1,1536,128]{2,1,0:T(8,128)(2,1)}, u32[]{:S(2)}) copy-start(bf16[1,1536,128]{2,1,0:T(8,128)(2,1)} %get-tuple-element.97) | copy-start | bytes 1179652
  495.4 4.9 copy-start.1
Sparse Core Ops, SparseCore 0:
  32.5 34.0 all-gather.2
  197.5 37.9 reduce-scatter.4
  238.2 28.1 reduce-scatter.8
  268.8 47.8 reduce-scatter.10
  319.8 29.8 reduce-scatter.6
  352.5 32.9 all-reduce.3
  389.9 102.3 all-reduce.5
